TPU v7x, 32 devices: a whole 2x2x4 slice. The times are simulated.
32 devices in a mesh: groups: 2 (over y), blk: 4 (over z), cells: 2 (over x), rep: 2 (over core).
Axes of the slice: x: 2, y: 2, z: 4, core: 2. Of those that a mesh axis runs over, the one named last changes fastest.
Arguments:
- probes: bfloat16 [32, 2, 4096], P('rep', 'cells', ('groups', 'blk')), parts along dimension 2, may hold values from -6 to 6
- depth_level: int32 [2, 4096], P('cells', ('groups', 'blk')), parts along dimension 1, may hold values from 0 to 15
- depth_scale: float32 [16], replicated, may hold values from 0.2 to 1.5
- sensitivity: bfloat16 [6, 3072, 2, 2048], P(None, ('groups', 'blk'), 'cells'), parts along dimension 1, may hold values from -0.125 to 0.125
- data_weight: float32 [6, 3072], P(None, ('groups', 'blk')), parts along dimension 1, may hold values from 0.05 to 0.5
- face_first: int32 [2, 2048], P('cells', ('groups', 'blk')), parts along dimension 1, may hold values from 0 to 2047, as said below
- face_second: int32 [2, 2048], P('cells', ('groups', 'blk')), parts along dimension 1, may hold values from 0 to 4095, as said below
- face_coef: float32 [2, 2048], P('cells', ('groups', 'blk')), parts along dimension 1, may hold values from 0.2 to 0.8
- face_count: int32 [2, 8], P('cells', ('groups', 'blk')), parts along dimension 1, may hold values from 51 to 256, as said below
Outputs:
- hessian_probe: float32 [32, 2, 4096], P('rep', 'cells', ('groups', 'blk')), parts along dimension 2
There are 2 independent parts, one for each index of `groups`. A program takes and returns all parts, laid end to end along the dimension named above; an argument that names none is the same for every part. Nothing has to cross between parts.
Inputs may be any that keep to these rules, and one draw needn't show every extreme that they name: `face_first`: a cell number within partition p. `face_second`: never equal to face_first of the same slot; values of 2048 or more name cells of the next partition, which the last partition never does. Only the first face_count[p, b] slots of block b of partition p (slots b * 256 onward) hold faces, the others are ignored; in every draw some block is full.
All inputs are finite; a program needn't handle non-finite values.
Results may differ from a plain program's by a relative error of at most 0.0029.
Values may be sent and summed in bfloat16 or wider, within the bound.
A program may use at most 64 MiB of HBM per device.

v0:
```python
import jax
import jax.numpy as jnp
from jax import lax
from jax.sharding import PartitionSpec as P


def shifted(block, axis, distance):
    devices = range(lax.axis_size(axis))
    route = [(i - distance, i) for i in devices if i - distance in devices]
    return lax.ppermute(block, axis, route)


def level_scale(depth_level, depth_scale):
    levels = jnp.arange(depth_scale.shape[0], dtype=jnp.int32)
    pick_rows = (depth_level[..., None] == levels).astype(jnp.float32)
    return jnp.sum(pick_rows * depth_scale, axis=-1)


def pick_hot(indices, offset, count):
    return (indices[:, None] - offset == jnp.arange(count, dtype=jnp.int32)[None, :]).astype(
        jnp.bfloat16
    )


def pick_values(block, hot):
    dims = (((1,), (1,)), ((), ()))
    return lax.dot_general(block, hot, dims, preferred_element_type=jnp.float32)


def spread_flux(flux, hot):
    upper = flux.astype(jnp.bfloat16)
    lower = (flux - upper.astype(jnp.float32)).astype(jnp.bfloat16)
    return jnp.dot(upper, hot, preferred_element_type=jnp.float32) + jnp.dot(
        lower, hot, preferred_element_type=jnp.float32
    )


def on_device(
    probes,
    depth_level,
    depth_scale,
    sensitivity,
    data_weight,
    face_first,
    face_second,
    face_coef,
    face_count,
):
    own_scale = level_scale(depth_level, depth_scale)
    weighted = (probes.astype(jnp.float32) * own_scale[None]).astype(jnp.bfloat16)
    probe_block = lax.all_gather(weighted, "blk", axis=2, tiled=True)
    slot_count = face_first.shape[1]
    live_all = (jnp.arange(slot_count, dtype=jnp.int32) < face_count[0, 0]).astype(jnp.float32)
    matrix = sensitivity[:, :, 0, :]
    first_cell = face_first[0]
    second_cell = face_second[0]
    coef_slots = face_coef[0]
    probe_cols = probe_block[:, 0, :]
    part_cells = probe_cols.shape[1]
    partial_value = jnp.einsum(
        "msc,qc->qms", matrix, probe_cols, preferred_element_type=jnp.float32
    )
    predicted = lax.psum(partial_value, "cells")
    residual = (data_weight[None] * predicted).astype(jnp.bfloat16)
    adjoint = jnp.einsum("msc,qms->qc", matrix, residual, preferred_element_type=jnp.float32)
    first_hot = pick_hot(first_cell, 0, part_cells)
    second_own = pick_hot(second_cell, 0, part_cells)
    first_val = pick_values(probe_cols, first_hot)
    second_val = pick_values(probe_cols, second_own)
    crossing = (second_cell >= part_cells).astype(jnp.float32)
    asked = shifted(second_cell, "cells", 1)
    asked_hot = pick_hot(asked, part_cells, part_cells)
    answer = pick_values(probe_cols, asked_hot).astype(jnp.bfloat16)
    received = shifted(answer, "cells", -1)
    second_val = second_val + crossing * received.astype(jnp.float32)
    flux_term = coef_slots * (coef_slots * live_all * (first_val - second_val))
    own_term = spread_flux(flux_term, first_hot) - spread_flux(flux_term, second_own)
    sent_flux = shifted(flux_term * crossing, "cells", 1)
    arrived = -spread_flux(sent_flux, asked_hot)
    total_term = (adjoint + own_term + arrived)[:, None, :]
    result = lax.psum_scatter(total_term, "blk", scatter_dimension=2, tiled=True)
    return result * own_scale[None]


def solution(mesh):
    return jax.shard_map(
        on_device,
        mesh=mesh,
        in_specs=(
            P("rep", "cells", ("groups", "blk")),
            P("cells", ("groups", "blk")),
            P(),
            P(None, ("groups", "blk"), "cells", None),
            P(None, ("groups", "blk")),
            P("cells", ("groups", "blk")),
            P("cells", ("groups", "blk")),
            P("cells", ("groups", "blk")),
            P("cells", ("groups", "blk")),
        ),
        out_specs=P("rep", "cells", ("groups", "blk")),
        check_vma=False,
    )
```

profile of v0, /device:TPU:0, one launch (start us, length us, event | category | flops | bytes accessed | tf_op | source)
XLA Modules:
  0.0 87.3 jit_solution(1859797593118502068)
XLA Ops:
  6.5 0.0 all-reduce.2.cloned.1.call-start
  6.5 0.8 select_reduce_fusion
  7.3 0.7 multiply_convert_fusion.2
  8.0 14.9 %all_gather.3 = bf16[16,1,2048]{2,0,1:T(8,128)(2,1)S(1)} all-gather(bf16[16,1,512]{2,0,1:T(8,128)(2,1)S(1)} %multiply_convert_fusion.2), channel_id=1, replica_groups=mesh['groups'=2,'blk'=4,'cells'=2,'rep'=2] {'blk'}, dimensions={2}, use_global_device_ids=true | all-gather | bytes 81920 | tf_op jit(solution)/shard_map/all_gather | solution.py:51
  22.9 0.0 copy-start.2
  22.9 0.0 copy-start.3
  22.9 0.0 copy-start.1
  22.9 6.9 %fusion.2 = f32[16,6,384]{2,0,1:T(8,128)} fusion(bf16[6,384,1,2048]{3,1,2,0:T(8,128)(2,1)} %param.12, bf16[16,1,2048]{2,0,1:T(8,128)(2,1)S(1)} %all_gather.3), kind=kOutput, calls=%fused_computation.2 | convolution fusion | flops 150994944 | bytes 9650176 | tf_op jit(solution)/shard_map/msc,qc->qms/dot_general | solution.py:60
  29.9 0.0 all-reduce.2.cloned.1.call-update
  29.9 0.0 copy-start
  29.9 0.0 reduce-scatter.2.cloned.1.call-start
  30.0 0.0 copy-done.2
  30.0 3.4 %collective-permute-start = (s32[256]{0:T(256)S(1)}, s32[256]{0:T(256)S(1)}, u32[]{:S(2)}, u32[]{:S(2)}) collective-permute-start(s32[256]{0:T(256)S(1)} %bitcast.33), channel_id=1, source_target_pairs={{0,2},{1,3},{4,6},{5,7},{8,10},{9,11},{12,14},{13,15},{16,18},{17,... | collective-permute-start | bytes 3080 | tf_op jit(solution)/shard_map/ppermute | solution.py:10
  33.4 0.5 fusion.15
  33.9 0.0 copy-done.3
  33.9 0.5 fusion.17
  35.0 0.0 collective-permute-done
  35.1 0.5 fusion.18
  35.5 1.3 %collective-permute-start.1 = (bf16[16,256]{1,0:T(8,128)(2,1)S(1)}, bf16[16,256]{1,0:T(8,128)(2,1)S(1)}, u32[]{:S(2)}, u32[]{:S(2)}) collective-permute-start(bf16[16,256]{1,0:T(8,128)(2,1)S(1)} %fusion.18), channel_id=1, source_target_pairs={{2,0},{3,1},{6,4},{7,5},{10,8},{11,9},{14,12},{15,13},{18,16},{19,... | collective-permute-start | bytes 24584 | tf_op jit(solution)/shard_map/ppermute | solution.py:10
  36.8 0.0 copy-done.1
  36.9 4.2 %collective-permute-done.1 = bf16[16,256]{1,0:T(8,128)(2,1)S(1)} collective-permute-done((bf16[16,256]{1,0:T(8,128)(2,1)S(1)}, bf16[16,256]{1,0:T(8,128)(2,1)S(1)}, u32[]{:S(2)}, u32[]{:S(2)}) %collective-permute-start.1) | collective-permute-done | bytes 8224 | tf_op jit(solution)/shard_map/ppermute | solution.py:10
  41.1 0.5 fusion.16
  41.6 0.5 convolution_add_fusion.2
  42.1 1.6 %collective-permute-start.2 = (f32[16,256]{1,0:T(8,128)S(1)}, f32[16,256]{1,0:T(8,128)S(1)}, u32[]{:S(2)}, u32[]{:S(2)}) collective-permute-start(f32[16,256]{1,0:T(8,128)S(1)} %get-tuple-element.5), channel_id=1, source_target_pairs={{0,2},{1,3},{4,6},{5,7},{8,10},{9,11},{12,14},{13,15},{16,18},{17,... | collective-permute-start | bytes 49160 | tf_op jit(solution)/shard_map/ppermute | solution.py:10
  43.7 0.5 fusion.14
  44.2 0.9 %collective-permute-done.2 = f32[16,256]{1,0:T(8,128)S(1)} collective-permute-done((f32[16,256]{1,0:T(8,128)S(1)}, f32[16,256]{1,0:T(8,128)S(1)}, u32[]{:S(2)}, u32[]{:S(2)}) %collective-permute-start.2) | collective-permute-done | bytes 16416 | tf_op jit(solution)/shard_map/ppermute | solution.py:10
  45.2 0.5 fusion.12
  45.7 7.2 %all-reduce.2.cloned.1.call-done = f32[16,6,384]{2,0,1:T(8,128)} async-done(((f32[16,6,384]{2,0,1:T(8,128)}), f32[16,6,384]{2,0,1:T(8,128)}) %all-reduce.2.cloned.1.call-update) | async-done | bytes 147472 | tf_op jit(solution)/shard_map/psum | solution.py:63
  52.9 0.0 copy-done
  52.9 5.1 %fusion.4 = f32[16,2048]{1,0:T(8,128)S(1)} fusion(bf16[6,384,1,2048]{3,1,2,0:T(8,128)(2,1)} %param.12, f32[16,6,384]{2,0,1:T(8,128)} %all-reduce.2.cloned.1.call-done, f32[6,384]{1,0:T(8,128)S(1)} %copy-done), kind=kOutput, calls=%fused_computation.4 | convolution fusion | flops 151068672 | bytes 9724928 | tf_op jit(solution)/shard_map/msc,qms->qc/dot_general | solution.py:65
  58.0 0.5 fusion.11
  58.5 1.1 %fusion.9 = f32[16,1,2048]{2,0,1:T(8,128)} fusion(f32[16,2048]{1,0:T(8,128)S(1)} %fusion.11, f32[16,2048]{1,0:T(8,128)S(1)} %fusion.12, s32[256]{0:T(256)S(1)} %broadcast_add_fusion, f32[16,256]{1,0:T(8,128)S(1)} %collective-permute-done.2), kind=kOutput, calls=%fused_computation.8 | convolution fusion | flops 17403904 | bytes 410624 | tf_op jit(solution)/shard_map/dot_general | solution.py:33
  59.6 0.0 reduce-scatter.2.cloned.1.call-update
  59.7 19.4 %reduce-scatter.2.cloned.1.call-done = f32[16,1,512]{2,0,1:T(8,128)} async-done(((f32[16,1,2048]{2,0,1:T(8,128)}), f32[16,1,512]{2,0,1:T(8,128)}) %reduce-scatter.2.cloned.1.call-update) | async-done | bytes 32784 | tf_op jit(solution)/shard_map/reduce_scatter | solution.py:81
  79.1 0.8 broadcast_multiply_fusion
  79.8 0.6 copy.11
  (4 shorter events, 0.0 us)
Async XLA Ops:
  6.5 46.4 %all-reduce.2.cloned.1.call-start = ((), (), s32[]{:S(2)}) async-start(), calls=%async_computation.1 | async-start | bytes 294912 | tf_op jit(solution)/shard_map/psum | solution.py:63
  22.9 7.0 %copy-start.2 = (s32[1,256]{1,0:T(1,128)S(1)}, s32[1,256]{1,0:T(1,128)}, u32[]{:S(2)}) copy-start(s32[1,256]{1,0:T(1,128)} %param.15) | copy-start | bytes 3076
  22.9 10.9 %copy-start.3 = (s32[1,256]{1,0:T(1,128)S(1)}, s32[1,256]{1,0:T(1,128)}, u32[]{:S(2)}) copy-start(s32[1,256]{1,0:T(1,128)} %param.14) | copy-start | bytes 3076
  22.9 13.9 %copy-start.1 = (f32[1,256]{1,0:T(1,128)S(1)}, f32[1,256]{1,0:T(1,128)}, u32[]{:S(2)}) copy-start(f32[1,256]{1,0:T(1,128)} %param.16) | copy-start | bytes 3076
  29.9 23.0 %copy-start = (f32[6,384]{1,0:T(8,128)S(1)}, f32[6,384]{1,0:T(8,128)}, u32[]{:S(2)}) copy-start(f32[6,384]{1,0:T(8,128)} %param.13) | copy-start | bytes 27652
  29.9 49.2 %reduce-scatter.2.cloned.1.call-start = ((), (), s32[]{:S(2)}) async-start(), calls=%async_computation.2 | async-start | bytes 163840 | tf_op jit(solution)/shard_map/reduce_scatter | solution.py:81
  30.0 5.1 %collective-permute-start = (s32[256]{0:T(256)S(1)}, s32[256]{0:T(256)S(1)}, u32[]{:S(2)}, u32[]{:S(2)}) collective-permute-start(s32[256]{0:T(256)S(1)} %bitcast.33), channel_id=1, source_target_pairs={{0,2},{1,3},{4,6},{5,7},{8,10},{9,11},{12,14},{13,15},{16,18},{17,... | collective-permute-start | bytes 3080 | tf_op jit(solution)/shard_map/ppermute | solution.py:10
  35.5 5.5 %collective-permute-start.1 = (bf16[16,256]{1,0:T(8,128)(2,1)S(1)}, bf16[16,256]{1,0:T(8,128)(2,1)S(1)}, u32[]{:S(2)}, u32[]{:S(2)}) collective-permute-start(bf16[16,256]{1,0:T(8,128)(2,1)S(1)} %fusion.18), channel_id=1, source_target_pairs={{2,0},{3,1},{6,4},{7,5},{10,8},{11,9},{14,12},{15,13},{18,16},{19,... | collective-permute-start | bytes 24584 | tf_op jit(solution)/shard_map/ppermute | solution.py:10
  42.1 3.1 %collective-permute-start.2 = (f32[16,256]{1,0:T(8,128)S(1)}, f32[16,256]{1,0:T(8,128)S(1)}, u32[]{:S(2)}, u32[]{:S(2)}) collective-permute-start(f32[16,256]{1,0:T(8,128)S(1)} %get-tuple-element.5), channel_id=1, source_target_pairs={{0,2},{1,3},{4,6},{5,7},{8,10},{9,11},{12,14},{13,15},{16,18},{17,... | collective-permute-start | bytes 49160 | tf_op jit(solution)/shard_map/ppermute | solution.py:10
Sparse Core Ops, SparseCore 0:
  30.0 22.8 all-reduce.1
  59.8 19.2 reduce-scatter.1
where the time goes:
time: 87.7 us; the launch traced here: 87.3 us
  waiting for transfers between devices  31.8 us (36%)
  matrix products  17.1 us (19%)
  blocking collectives  14.9 us (17%)
  between operations  14.1 us (16%)
  starting transfers between devices  6.36 us (7%)
  other arithmetic  2.29 us (3%)
    reduce_scatter x1, waiting for transfers between devices, on_device(): lax.psum_scatter(total_term, 'blk', scatter_dimension=2, tiled=True)  19.4 us
    all_gather x1, blocking collectives, on_device(): probe_block = lax.all_gather(weighted, 'blk', axis=2, tiled=True)  14.9 us
    psum x1, waiting for transfers between devices, on_device(): predicted = lax.psum(partial_value, 'cells')  7.25 us
    dot_general x1, matrix products, on_device(): jnp.einsum('msc,qc->qms', matrix, probe_cols, preferred_element_type=jnp....  6.94 us
    ppermute x3, starting transfers between devices, shifted(): return lax.ppermute(block, axis, route)  6.32 us
    ppermute x3, waiting for transfers between devices, shifted(): return lax.ppermute(block, axis, route)  5.15 us
    dot_general x1, matrix products, on_device(): jnp.einsum('msc,qms->qc', matrix, residual, preferred_element_type=jnp.fl...  5.1 us
    dot_general x3, matrix products, spread_flux(): jnp.dot(upper, hot, preferred_element_type=jnp.float32)  2.14 us
  transfers between devices with their start and end apart: 5, of which 4 were waited for; matrix products, arithmetic and copies ran while one was open for 4% of the time, Pallas kernels for 0%

commit v1 on v0

--- a/solution.py
+++ b/solution.py
@@ -1,7 +1,15 @@
+import functools
+
 import jax
 import jax.numpy as jnp
 from jax import lax
+from jax.experimental import pallas as pl
+from jax.experimental.pallas import tpu as pltpu
 from jax.sharding import PartitionSpec as P
+
+CHUNKS = 3
+BUILD_ROWS = 256
+MESH = pl.DeviceIdType.MESH
 
 
 def shifted(block, axis, distance):
@@ -35,7 +43,7 @@
     )
 
 
-def on_device(
+def plain_form(
     probes,
     depth_level,
     depth_scale,
@@ -82,9 +90,320 @@
     return result * own_scale[None]
 
 
+NN = (((1,), (0,)), ((), ()))
+NT = (((1,), (1,)), ((), ()))
+
+
+def mxu(left, right, dims=NN):
+    return lax.dot_general(left, right, dims, preferred_element_type=jnp.float32)
+
+
+def in_two(value):
+    upper = value.astype(jnp.bfloat16)
+    lower = (value - upper.astype(jnp.float32)).astype(jnp.bfloat16)
+    return jnp.concatenate([upper, lower], axis=0)
+
+
+def fused_kernel(
+    nblk,
+    probes,
+    level,
+    table,
+    sens,
+    weight,
+    first,
+    second,
+    coef,
+    count,
+    out,
+    s_buf,
+    w_buf,
+    hot,
+    asked,
+    ans_send,
+    ans_recv,
+    flux_send,
+    flux_recv,
+    p_own,
+    p_send,
+    p_recv,
+    acc,
+    part_send,
+    part_recv,
+    load_sem,
+    ask_sem,
+    gather_sem,
+    ans_sem,
+    flux_sem,
+    p_sem,
+    part_sem,
+):
+    blk = lax.axis_index("blk")
+    other = 1 - lax.axis_index("cells")
+    probe_count, own_cells = probes.shape
+    part_cells = w_buf.shape[1]
+    slots = first.shape[1]
+    chunk_rows = s_buf.shape[0] // CHUNKS
+    comps, stations = weight.shape
+    per_chunk = comps // CHUNKS
+
+    def block(index):
+        return pl.ds(pl.multiple_of(index * own_cells, own_cells), own_cells)
+
+    def rows(k):
+        return pl.ds(k * chunk_rows, chunk_rows)
+
+    def to_blk(src, dst, sem, d):
+        return pltpu.make_async_remote_copy(
+            src_ref=src,
+            dst_ref=dst,
+            send_sem=sem.at[0, d - 1],
+            recv_sem=sem.at[1, d - 1],
+            device_id={"blk": lax.rem(blk + d, nblk)},
+            device_id_type=MESH,
+        )
+
+    def to_other(src, dst, sem, k=0):
+        return pltpu.make_async_remote_copy(
+            src_ref=src,
+            dst_ref=dst,
+            send_sem=sem.at[0, k],
+            recv_sem=sem.at[1, k],
+            device_id={"cells": other},
+            device_id_type=MESH,
+        )
+
+    barrier = pltpu.get_barrier_semaphore()
+    for d in range(1, nblk):
+        pl.semaphore_signal(
+            barrier, inc=1, device_id={"blk": lax.rem(blk + d, nblk)}, device_id_type=MESH
+        )
+    pl.semaphore_signal(barrier, inc=1, device_id={"cells": other}, device_id_type=MESH)
+
+    loads = [
+        pltpu.make_async_copy(sens.at[rows(k), :], s_buf.at[rows(k), :], load_sem.at[k])
+        for k in range(CHUNKS)
+    ]
+    for load in loads:
+        load.start()
+
+    levels = level[...]
+    scale = jnp.zeros(levels.shape, jnp.float32)
+    for index in range(table.shape[0]):
+        scale = jnp.where(levels == index, table[index], scale)
+    weighted = (probes[...].astype(jnp.float32) * scale).astype(jnp.bfloat16)
+    w_buf[:, block(blk)] = weighted
+
+    pl.semaphore_wait(barrier, nblk)
+    gathers = [
+        to_blk(w_buf.at[:, block(blk)], w_buf.at[:, block(blk)], gather_sem, d)
+        for d in range(1, nblk)
+    ]
+    for copy in gathers:
+        copy.start()
+    ask = to_other(second, asked, ask_sem)
+    ask.start()
+
+    first_row = first[...]
+    second_row = second[...]
+    cell_in = lax.broadcasted_iota(jnp.int32, (BUILD_ROWS, slots), 0)
+
+    def build_own(step, carry):
+        base = pl.multiple_of(step * BUILD_ROWS, BUILD_ROWS)
+        one = jnp.where(cell_in == first_row - base, 1.0, 0.0)
+        both = jnp.where(cell_in == second_row - base, -1.0, one)
+        hot[pl.ds(base, BUILD_ROWS), pl.ds(0, slots)] = both.astype(jnp.bfloat16)
+        return carry
+
+    lax.fori_loop(0, part_cells // BUILD_ROWS, build_own, 0)
+    ask.wait_recv()
+    asked_row = asked[...] - part_cells
+
+    def build_asked(step, carry):
+        base = pl.multiple_of(step * BUILD_ROWS, BUILD_ROWS)
+        one = jnp.where(cell_in == asked_row - base, 1.0, 0.0)
+        hot[pl.ds(base, BUILD_ROWS), pl.ds(slots, slots)] = one.astype(jnp.bfloat16)
+        return carry
+
+    lax.fori_loop(0, part_cells // BUILD_ROWS, build_asked, 0)
+
+    for copy in gathers:
+        copy.wait_recv()
+    cols = w_buf[...]
+    ans_send[...] = mxu(cols, hot[:, slots:]).astype(jnp.bfloat16)
+    answer = to_other(ans_send, ans_recv, ans_sem)
+    answer.start()
+
+    swaps = []
+    for k in range(CHUNKS):
+        loads[k].wait()
+        partial = mxu(cols, s_buf[rows(k), :], NT)
+        p_own[:, rows(k)] = partial
+        p_send[k] = partial.astype(jnp.bfloat16)
+        swap = to_other(p_send.at[k], p_recv.at[k], p_sem, k)
+        swap.start()
+        swaps.append(swap)
+
+    jump = mxu(cols, hot[:, :slots])
+    crossing = jnp.where(second_row >= part_cells, 1.0, 0.0)
+    live = jnp.where(lax.broadcasted_iota(jnp.int32, (1, slots), 1) < count[0, 0], 1.0, 0.0)
+    coef_row = coef[...]
+    answer.wait_recv()
+    jump = jump - crossing * ans_recv[...].astype(jnp.float32)
+    flux = coef_row * (coef_row * live * jump)
+    flux_send[...] = -(flux * crossing)
+    forward = to_other(flux_send, flux_recv, flux_sem)
+    forward.start()
+    flux_pair = in_two(flux)
+
+    def residual_of(k):
+        predicted = p_own[:, rows(k)] + p_recv[k].astype(jnp.float32)
+        factor = jnp.concatenate(
+            [weight[pl.ds(k * per_chunk + i, 1), :] for i in range(per_chunk)], axis=1
+        )
+        return (factor * predicted).astype(jnp.bfloat16)
+
+    for k in range(CHUNKS - 1):
+        swaps[k].wait_recv()
+        term = mxu(residual_of(k), s_buf[rows(k), :])
+        if k == 0:
+            acc[...] = term
+        else:
+            acc[...] += term
+
+    forward.wait_recv()
+    pairs = jnp.concatenate([flux_pair, in_two(flux_recv[...])], axis=1)
+    swaps[-1].wait_recv()
+    last = residual_of(CHUNKS - 1)
+    sums = []
+    total = None
+    for d in list(range(1, nblk)) + [0]:
+        here = block(lax.rem(blk + d, nblk))
+        spread = mxu(pairs, hot[here, :], NT)
+        term = (
+            acc[:, here]
+            + mxu(last, s_buf[rows(CHUNKS - 1), here])
+            + (spread[:probe_count] + spread[probe_count:])
+        )
+        if d:
+            part_send[d - 1] = term.astype(jnp.bfloat16)
+            copy = to_blk(part_send.at[d - 1], part_recv.at[d - 1], part_sem, d)
+            copy.start()
+            sums.append(copy)
+        else:
+            total = term
+    for d in range(1, nblk):
+        sums[d - 1].wait_recv()
+        total = total + part_recv[d - 1].astype(jnp.float32)
+    out[...] = total * scale
+
+    for copy in gathers + [ask, answer, forward] + swaps + sums:
+        copy.wait_send()
+
+
+def fused_form(
+    nblk,
+    probes,
+    depth_level,
+    depth_scale,
+    sensitivity,
+    data_weight,
+    face_first,
+    face_second,
+    face_coef,
+    face_count,
+):
+    probe_count, _, own_cells = probes.shape
+    comps, stations, _, part_cells = sensitivity.shape
+    rows = comps * stations
+    slots = face_first.shape[1]
+    matrix = sensitivity[:, :, 0, :].reshape(rows, part_cells)
+    vmem = pl.BlockSpec(memory_space=pltpu.VMEM)
+    smem = pl.BlockSpec(memory_space=pltpu.SMEM)
+    bf16, f32 = jnp.bfloat16, jnp.float32
+    dma = pltpu.SemaphoreType.DMA
+    result = pl.pallas_call(
+        functools.partial(fused_kernel, nblk),
+        out_shape=jax.ShapeDtypeStruct((probe_count, own_cells), f32),
+        in_specs=[
+            vmem,
+            vmem,
+            smem,
+            pl.BlockSpec(memory_space=pl.ANY),
+            vmem,
+            vmem,
+            vmem,
+            vmem,
+            smem,
+        ],
+        out_specs=vmem,
+        scratch_shapes=[
+            pltpu.VMEM((rows, part_cells), bf16),
+            pltpu.VMEM((probe_count, part_cells), bf16),
+            pltpu.VMEM((part_cells, 2 * slots), bf16),
+            pltpu.VMEM((1, slots), jnp.int32),
+            pltpu.VMEM((probe_count, slots), bf16),
+            pltpu.VMEM((probe_count, slots), bf16),
+            pltpu.VMEM((probe_count, slots), f32),
+            pltpu.VMEM((probe_count, slots), f32),
+            pltpu.VMEM((probe_count, rows), f32),
+            pltpu.VMEM((CHUNKS, probe_count, rows // CHUNKS), bf16),
+            pltpu.VMEM((CHUNKS, probe_count, rows // CHUNKS), bf16),
+            pltpu.VMEM((probe_count, part_cells), f32),
+            pltpu.VMEM((nblk - 1, probe_count, own_cells), bf16),
+            pltpu.VMEM((nblk - 1, probe_count, own_cells), bf16),
+            dma((CHUNKS,)),
+            dma((2, 1)),
+            dma((2, nblk - 1)),
+            dma((2, 1)),
+            dma((2, 1)),
+            dma((2, CHUNKS)),
+            dma((2, nblk - 1)),
+        ],
+        compiler_params=pltpu.CompilerParams(
+            collective_id=0, has_side_effects=True, vmem_limit_bytes=56 * 2**20
+        ),
+        cost_estimate=pl.CostEstimate(
+            flops=4 * probe_count * rows * part_cells,
+            bytes_accessed=2 * rows * part_cells,
+            transcendentals=0,
+        ),
+    )(
+        probes[:, 0, :],
+        depth_level,
+        depth_scale,
+        matrix,
+        data_weight,
+        face_first,
+        face_second,
+        face_coef,
+        face_count,
+    )
+    return result[:, None, :]
+
+
+def fits_kernel(nblk, ncells, probes, sensitivity):
+    own_cells = probes.shape[2]
+    comps, stations, _, part_cells = sensitivity.shape
+    return (
+        ncells == 2
+        and own_cells % 128 == 0
+        and part_cells % BUILD_ROWS == 0
+        and stations % 128 == 0
+        and comps % CHUNKS == 0
+        and probes.shape[0] % 16 == 0
+    )
+
+
+def on_device(nblk, ncells, *arrays):
+    if fits_kernel(nblk, ncells, arrays[0], arrays[3]):
+        return fused_form(nblk, *arrays)
+    return plain_form(*arrays)
+
+
 def solution(mesh):
     return jax.shard_map(
-        on_device,
+        functools.partial(on_device, mesh.shape["blk"], mesh.shape["cells"]),
         mesh=mesh,
         in_specs=(
             P("rep", "cells", ("groups", "blk")),

time: 87.7 us -> 24.6 us (0.28)
  waiting for transfers between devices: 31.8 us -> 0 us
  Pallas kernels: 0 us -> 22.3 us
  matrix products: 17.1 us -> 0 us
  blocking collectives: 14.9 us -> 0 us
  between operations: 14.1 us -> 0.66 us
  starting transfers between devices: 6.36 us -> 0 us
  other arithmetic: 2.29 us -> 0 us
    pallas_call x0 -> x1, Pallas kernels: none -> 22.3 us  [fused_form(): pl.pallas_call(functools.partial(fused_kernel, nblk), out_shape=jax.Shape...]
    reduce_scatter x1 -> x0, waiting for transfers between devices: 19.4 us -> none  [on_device(): lax.psum_scatter(total_term, 'blk', scatter_dimension=2, tiled=True)]
    dot_general x11 -> x0, matrix products: 17.1 us -> none  [the longest x1 6.94 us: on_device(): jnp.einsum('msc,qc->qms', matrix, probe_cols, preferred_element_type=jnp....]
    all_gather x1 -> x0, blocking collectives: 14.9 us -> none  [on_device(): probe_block = lax.all_gather(weighted, 'blk', axis=2, tiled=True)]
    psum x1 -> x0, waiting for transfers between devices: 7.25 us -> none  [on_device(): predicted = lax.psum(partial_value, 'cells')]
    ppermute x3 -> x0, starting transfers between devices: 6.32 us -> none  [shifted(): return lax.ppermute(block, axis, route)]
    ppermute x3 -> x0, waiting for transfers between devices: 5.15 us -> none  [shifted(): return lax.ppermute(block, axis, route)]
    broadcast_in_dim x0 -> x1, local copies, waits for them, and re-layouts: none -> 1.41 us  [fused_form(): return result[:, None, :]]
  transfers between devices with their start and end apart: 5 -> 0, of which waited for: 4 -> 0; matrix products, arithmetic and copies ran while one was open for 4% -> 0% of each run, Pallas kernels for 0% -> 0%
where the time goes in v1:
time: 24.6 us; the launch traced here: 24.4 us
  Pallas kernels  22.3 us (91%)
  local copies, waits for them, and re-layouts  1.41 us (6%)
  between operations  0.66 us (3%)
    pallas_call x1, Pallas kernels, fused_form(): pl.pallas_call(functools.partial(fused_kernel, nblk), out_shape=jax.Shape...  22.3 us
    broadcast_in_dim x1, local copies, waits for them, and re-layouts, fused_form(): return result[:, None, :]  1.41 us

profile of v1, /device:TPU:0, one launch (start us, length us, event | category | flops | bytes accessed | tf_op | source)
XLA Modules:
  0.0 24.4 jit_solution(16927170646132659046)
XLA Ops:
  0.7 22.3 %shard_map.91 = f32[16,512]{1,0:T(8,128)} custom-call(bf16[16,512]{1,0:T(8,128)(2,1)} %bitcast.5, s32[1,512]{1,0:T(1,128)} %level.1, f32[16]{0:T(128)} %table.1, bf16[2304,2048]{1,0:T(8,128)(2,1)} %bitcast.3, f32[6,384]{1,0:T(8,128)} %weight.1, s32[1,256]{1,0:T(1,128)} %first.1, s32[1,256]{1,0:T(1,128)} %second.1, f32[1,256]{1,0:T(1,128)} %coef.1, ...), custom_call_target="tpu_custom_call" | custom-call | flops 301989888 | bytes 9437184 | tf_op jit(solution)/shard_map/pallas_call | solution.py:325
  23.0 1.4 %copy.10 = f32[16,1,512]{2,1,0:T(1,128)} copy(f32[16,1,512]{2,0,1:T(8,128)} %bitcast.4) | data formatting | bytes 65536 | tf_op jit(solution)/shard_map/broadcast_in_dim | solution.py:382

commit v2 on v1

--- a/solution.py
+++ b/solution.py
@@ -105,39 +105,48 @@
 
 
 def fused_kernel(
-    nblk,
+    probes_in,
+    level_in,
+    table_in,
+    sens,
+    weight_in,
+    first_in,
+    second_in,
+    coef_in,
+    count_in,
+    out,
     probes,
     level,
     table,
-    sens,
     weight,
     first,
     second,
     coef,
     count,
-    out,
     s_buf,
     w_buf,
     hot,
+    strength,
     asked,
-    ans_send,
-    ans_recv,
-    flux_send,
-    flux_recv,
+    asked_strength,
+    val_send,
+    val_recv,
+    val_own,
     p_own,
     p_send,
     p_recv,
     acc,
     part_send,
     part_recv,
+    small_sem,
     load_sem,
     ask_sem,
     gather_sem,
-    ans_sem,
-    flux_sem,
+    val_sem,
     p_sem,
     part_sem,
 ):
+    nblk = 4
     blk = lax.axis_index("blk")
     other = 1 - lax.axis_index("cells")
     probe_count, own_cells = probes.shape
@@ -146,6 +155,12 @@
     chunk_rows = s_buf.shape[0] // CHUNKS
     comps, stations = weight.shape
     per_chunk = comps // CHUNKS
+    half = blk // 2
+
+    def mirrored(place):
+        return place + half * (nblk - 1 - 2 * place)
+
+    peers = [mirrored(1 - mirrored(blk)), mirrored(2), mirrored(3)]
 
     def block(index):
         return pl.ds(pl.multiple_of(index * own_cells, own_cells), own_cells)
@@ -153,13 +168,13 @@
     def rows(k):
         return pl.ds(k * chunk_rows, chunk_rows)
 
-    def to_blk(src, dst, sem, d):
+    def to_blk(src, dst, sem, arrival, peer):
         return pltpu.make_async_remote_copy(
             src_ref=src,
             dst_ref=dst,
-            send_sem=sem.at[0, d - 1],
-            recv_sem=sem.at[1, d - 1],
-            device_id={"blk": lax.rem(blk + d, nblk)},
+            send_sem=sem.at[0, peer],
+            recv_sem=sem.at[1, arrival],
+            device_id={"blk": peer},
             device_id_type=MESH,
         )
 
@@ -174,18 +189,33 @@
         )
 
     barrier = pltpu.get_barrier_semaphore()
-    for d in range(1, nblk):
-        pl.semaphore_signal(
-            barrier, inc=1, device_id={"blk": lax.rem(blk + d, nblk)}, device_id_type=MESH
-        )
+    for peer in reversed(peers):
+        pl.semaphore_signal(barrier, inc=1, device_id={"blk": peer}, device_id_type=MESH)
     pl.semaphore_signal(barrier, inc=1, device_id={"cells": other}, device_id_type=MESH)
 
+    pairs_in = [
+        (level_in, level),
+        (table_in, table),
+        (probes_in, probes),
+        (first_in, first),
+        (second_in, second),
+        (coef_in, coef),
+        (count_in, count),
+        (weight_in, weight),
+    ]
+    smalls = [
+        pltpu.make_async_copy(src, dst, small_sem.at[n]) for n, (src, dst) in enumerate(pairs_in)
+    ]
+    for copy in smalls:
+        copy.start()
     loads = [
         pltpu.make_async_copy(sens.at[rows(k), :], s_buf.at[rows(k), :], load_sem.at[k])
         for k in range(CHUNKS)
     ]
-    for load in loads:
-        load.start()
+    for copy in loads:
+        copy.start()
+    for copy in smalls:
+        copy.wait()
 
     levels = level[...]
     scale = jnp.zeros(levels.shape, jnp.float32)
@@ -193,68 +223,64 @@
         scale = jnp.where(levels == index, table[index], scale)
     weighted = (probes[...].astype(jnp.float32) * scale).astype(jnp.bfloat16)
     w_buf[:, block(blk)] = weighted
+    live = lax.broadcasted_iota(jnp.int32, (1, slots), 1) < count[...]
+    own_strength = jnp.where(live, coef[...], 0.0)
+    strength[...] = own_strength
 
     pl.semaphore_wait(barrier, nblk)
-    gathers = [
-        to_blk(w_buf.at[:, block(blk)], w_buf.at[:, block(blk)], gather_sem, d)
-        for d in range(1, nblk)
-    ]
+    mine = w_buf.at[:, block(blk)]
+    gathers = [to_blk(mine, mine, gather_sem, blk, peer) for peer in reversed(peers)]
     for copy in gathers:
         copy.start()
-    ask = to_other(second, asked, ask_sem)
-    ask.start()
-
-    first_row = first[...]
+    asks = [to_other(second, asked, ask_sem, 0), to_other(strength, asked_strength, ask_sem, 1)]
+    for copy in asks:
+        copy.start()
+
+    cell_in = lax.broadcasted_iota(jnp.int32, (BUILD_ROWS, slots), 0)
+
+    def mark(cells, part):
+        def build(step, carry):
+            base = pl.multiple_of(step * BUILD_ROWS, BUILD_ROWS)
+            one = jnp.where(cell_in == cells - base, 1.0, 0.0)
+            hot[pl.ds(base, BUILD_ROWS), pl.ds(part * slots, slots)] = one.astype(jnp.bfloat16)
+            return carry
+
+        lax.fori_loop(0, part_cells // BUILD_ROWS, build, 0)
+
     second_row = second[...]
-    cell_in = lax.broadcasted_iota(jnp.int32, (BUILD_ROWS, slots), 0)
-
-    def build_own(step, carry):
-        base = pl.multiple_of(step * BUILD_ROWS, BUILD_ROWS)
-        one = jnp.where(cell_in == first_row - base, 1.0, 0.0)
-        both = jnp.where(cell_in == second_row - base, -1.0, one)
-        hot[pl.ds(base, BUILD_ROWS), pl.ds(0, slots)] = both.astype(jnp.bfloat16)
-        return carry
-
-    lax.fori_loop(0, part_cells // BUILD_ROWS, build_own, 0)
-    ask.wait_recv()
-    asked_row = asked[...] - part_cells
-
-    def build_asked(step, carry):
-        base = pl.multiple_of(step * BUILD_ROWS, BUILD_ROWS)
-        one = jnp.where(cell_in == asked_row - base, 1.0, 0.0)
-        hot[pl.ds(base, BUILD_ROWS), pl.ds(slots, slots)] = one.astype(jnp.bfloat16)
-        return carry
-
-    lax.fori_loop(0, part_cells // BUILD_ROWS, build_asked, 0)
-
-    for copy in gathers:
-        copy.wait_recv()
-    cols = w_buf[...]
-    ans_send[...] = mxu(cols, hot[:, slots:]).astype(jnp.bfloat16)
-    answer = to_other(ans_send, ans_recv, ans_sem)
-    answer.start()
-
-    swaps = []
+    mark(first[...], 0)
+    mark(second_row, 1)
     for k in range(CHUNKS):
         loads[k].wait()
-        partial = mxu(cols, s_buf[rows(k), :], NT)
-        p_own[:, rows(k)] = partial
-        p_send[k] = partial.astype(jnp.bfloat16)
-        swap = to_other(p_send.at[k], p_recv.at[k], p_sem, k)
-        swap.start()
-        swaps.append(swap)
-
-    jump = mxu(cols, hot[:, :slots])
-    crossing = jnp.where(second_row >= part_cells, 1.0, 0.0)
-    live = jnp.where(lax.broadcasted_iota(jnp.int32, (1, slots), 1) < count[0, 0], 1.0, 0.0)
-    coef_row = coef[...]
-    answer.wait_recv()
-    jump = jump - crossing * ans_recv[...].astype(jnp.float32)
-    flux = coef_row * (coef_row * live * jump)
-    flux_send[...] = -(flux * crossing)
-    forward = to_other(flux_send, flux_recv, flux_sem)
-    forward.start()
-    flux_pair = in_two(flux)
+        p_own[:, rows(k)] = mxu(weighted, s_buf[rows(k), block(blk)], NT)
+    for copy in asks:
+        copy.wait_recv()
+    mark(asked[...] - part_cells, 2)
+    val_own[...] = mxu(weighted, hot[block(blk), :])
+
+    swaps = []
+    for place, peer in enumerate(peers):
+        theirs = w_buf.at[:, block(peer)]
+        to_blk(theirs, theirs, gather_sem, peer, peer).wait_recv()
+        cols = w_buf[:, block(peer)]
+        value = val_own[...] + mxu(cols, hot[block(peer), :])
+        if place < nblk - 2:
+            val_own[...] = value
+        else:
+            first_val = value[:, :slots]
+            second_val = value[:, slots : 2 * slots]
+            answer = value[:, 2 * slots :]
+            val_send[...] = jnp.concatenate([first_val, answer], axis=1).astype(jnp.bfloat16)
+            trade = to_other(val_send, val_recv, val_sem)
+            trade.start()
+        for k in range(CHUNKS):
+            partial = p_own[:, rows(k)] + mxu(cols, s_buf[rows(k), block(peer)], NT)
+            p_own[:, rows(k)] = partial
+            if place == nblk - 2:
+                p_send[k] = partial.astype(jnp.bfloat16)
+                swap = to_other(p_send.at[k], p_recv.at[k], p_sem, k)
+                swap.start()
+                swaps.append(swap)
 
     def residual_of(k):
         predicted = p_own[:, rows(k)] + p_recv[k].astype(jnp.float32)
@@ -263,42 +289,43 @@
         )
         return (factor * predicted).astype(jnp.bfloat16)
 
-    for k in range(CHUNKS - 1):
-        swaps[k].wait_recv()
-        term = mxu(residual_of(k), s_buf[rows(k), :])
-        if k == 0:
-            acc[...] = term
-        else:
-            acc[...] += term
-
-    forward.wait_recv()
-    pairs = jnp.concatenate([flux_pair, in_two(flux_recv[...])], axis=1)
-    swaps[-1].wait_recv()
-    last = residual_of(CHUNKS - 1)
+    crossing = jnp.where(second_row >= part_cells, 1.0, 0.0)
+    trade.wait_recv()
+    jump = first_val - second_val - crossing * val_recv[:, slots:].astype(jnp.float32)
+    flux = own_strength * (own_strength * jump)
+    far_strength = jnp.where(asked[...] >= part_cells, asked_strength[...], 0.0)
+    far_jump = val_recv[:, :slots].astype(jnp.float32) - answer
+    far_flux = far_strength * (far_strength * far_jump)
+    flux_pair = in_two(jnp.concatenate([flux, -flux, -far_flux], axis=1))
+    spread = mxu(flux_pair, hot[...], NT)
+    spread = spread[:probe_count] + spread[probe_count:]
+    swaps[0].wait_recv()
+    acc[...] = spread + mxu(residual_of(0), s_buf[rows(0), :])
+
+    for copy in swaps[1:]:
+        copy.wait_recv()
+    late = jnp.concatenate([residual_of(k) for k in range(1, CHUNKS)], axis=1)
+    late_rows = pl.ds(chunk_rows, (CHUNKS - 1) * chunk_rows)
     sums = []
-    total = None
-    for d in list(range(1, nblk)) + [0]:
-        here = block(lax.rem(blk + d, nblk))
-        spread = mxu(pairs, hot[here, :], NT)
-        term = (
-            acc[:, here]
-            + mxu(last, s_buf[rows(CHUNKS - 1), here])
-            + (spread[:probe_count] + spread[probe_count:])
-        )
-        if d:
-            part_send[d - 1] = term.astype(jnp.bfloat16)
-            copy = to_blk(part_send.at[d - 1], part_recv.at[d - 1], part_sem, d)
-            copy.start()
-            sums.append(copy)
-        else:
-            total = term
-    for d in range(1, nblk):
-        sums[d - 1].wait_recv()
-        total = total + part_recv[d - 1].astype(jnp.float32)
+    for place, peer in enumerate(reversed(peers)):
+        term = acc[:, block(peer)] + mxu(late, s_buf[late_rows, block(peer)])
+        part_send[place] = term.astype(jnp.bfloat16)
+        copy = to_blk(part_send.at[place], part_recv.at[blk], part_sem, blk, peer)
+        copy.start()
+        sums.append(copy)
+    total = acc[:, block(blk)] + mxu(late, s_buf[late_rows, block(blk)])
+    for peer in peers:
+        theirs = part_recv.at[peer]
+        to_blk(theirs, theirs, part_sem, peer, peer).wait_recv()
+        total = total + part_recv[peer].astype(jnp.float32)
     out[...] = total * scale
 
-    for copy in gathers + [ask, answer, forward] + swaps + sums:
+    for copy in gathers + asks + [trade] + swaps + sums:
         copy.wait_send()
+
+
+def hand_on(value, out):
+    out[:, 0, :] = value[...]
 
 
 def fused_form(
@@ -319,46 +346,44 @@
     slots = face_first.shape[1]
     matrix = sensitivity[:, :, 0, :].reshape(rows, part_cells)
     vmem = pl.BlockSpec(memory_space=pltpu.VMEM)
-    smem = pl.BlockSpec(memory_space=pltpu.SMEM)
-    bf16, f32 = jnp.bfloat16, jnp.float32
+    bf16, f32, i32 = jnp.bfloat16, jnp.float32, jnp.int32
     dma = pltpu.SemaphoreType.DMA
     result = pl.pallas_call(
-        functools.partial(fused_kernel, nblk),
+        fused_kernel,
         out_shape=jax.ShapeDtypeStruct((probe_count, own_cells), f32),
-        in_specs=[
-            vmem,
-            vmem,
-            smem,
-            pl.BlockSpec(memory_space=pl.ANY),
-            vmem,
-            vmem,
-            vmem,
-            vmem,
-            smem,
-        ],
+        in_specs=[pl.BlockSpec(memory_space=pl.ANY)] * 9,
         out_specs=vmem,
         scratch_shapes=[
+            pltpu.VMEM((probe_count, own_cells), bf16),
+            pltpu.VMEM((1, own_cells), i32),
+            pltpu.SMEM(depth_scale.shape, f32),
+            pltpu.VMEM((comps, stations), f32),
+            pltpu.VMEM((1, slots), i32),
+            pltpu.VMEM((1, slots), i32),
+            pltpu.VMEM((1, slots), f32),
+            pltpu.VMEM((1, 1), i32),
             pltpu.VMEM((rows, part_cells), bf16),
             pltpu.VMEM((probe_count, part_cells), bf16),
-            pltpu.VMEM((part_cells, 2 * slots), bf16),
-            pltpu.VMEM((1, slots), jnp.int32),
-            pltpu.VMEM((probe_count, slots), bf16),
-            pltpu.VMEM((probe_count, slots), bf16),
-            pltpu.VMEM((probe_count, slots), f32),
-            pltpu.VMEM((probe_count, slots), f32),
+            pltpu.VMEM((part_cells, 3 * slots), bf16),
+            pltpu.VMEM((1, slots), f32),
+            pltpu.VMEM((1, slots), i32),
+            pltpu.VMEM((1, slots), f32),
+            pltpu.VMEM((probe_count, 2 * slots), bf16),
+            pltpu.VMEM((probe_count, 2 * slots), bf16),
+            pltpu.VMEM((probe_count, 3 * slots), f32),
             pltpu.VMEM((probe_count, rows), f32),
             pltpu.VMEM((CHUNKS, probe_count, rows // CHUNKS), bf16),
             pltpu.VMEM((CHUNKS, probe_count, rows // CHUNKS), bf16),
             pltpu.VMEM((probe_count, part_cells), f32),
             pltpu.VMEM((nblk - 1, probe_count, own_cells), bf16),
-            pltpu.VMEM((nblk - 1, probe_count, own_cells), bf16),
+            pltpu.VMEM((nblk, probe_count, own_cells), bf16),
+            dma((8,)),
             dma((CHUNKS,)),
-            dma((2, 1)),
-            dma((2, nblk - 1)),
-            dma((2, 1)),
+            dma((2, 2)),
+            dma((2, nblk)),
             dma((2, 1)),
             dma((2, CHUNKS)),
-            dma((2, nblk - 1)),
+            dma((2, nblk)),
         ],
         compiler_params=pltpu.CompilerParams(
             collective_id=0, has_side_effects=True, vmem_limit_bytes=56 * 2**20
@@ -379,14 +404,20 @@
         face_coef,
         face_count,
     )
-    return result[:, None, :]
+    return pl.pallas_call(
+        hand_on,
+        out_shape=jax.ShapeDtypeStruct((probe_count, 1, own_cells), f32),
+        in_specs=[vmem],
+        out_specs=vmem,
+    )(result)
 
 
 def fits_kernel(nblk, ncells, probes, sensitivity):
     own_cells = probes.shape[2]
     comps, stations, _, part_cells = sensitivity.shape
     return (
-        ncells == 2
+        nblk == 4
+        and ncells == 2
         and own_cells % 128 == 0
         and part_cells % BUILD_ROWS == 0
         and stations % 128 == 0

time: 24.6 us -> 22.8 us (0.927)
  local copies, waits for them, and re-layouts: 1.41 us -> 0 us
  Pallas kernels: 22.3 us -> 22 us
    broadcast_in_dim x1 -> x0, local copies, waits for them, and re-layouts: 1.41 us -> none  [fused_form(): return result[:, None, :]]
    pallas_call x1 -> x2, Pallas kernels: 22.3 us -> 22 us  [the longest x1 20.6 us: fused_form(): pl.pallas_call(fused_kernel, out_shape=jax.ShapeDtypeStruct((probe_count,...]
where the time goes in v2:
time: 22.8 us; the launch traced here: 22.6 us
  Pallas kernels  22 us (96%)
  between operations  0.66 us (3%)
    pallas_call x1, Pallas kernels, fused_form(): pl.pallas_call(fused_kernel, out_shape=jax.ShapeDtypeStruct((probe_count,...  20.6 us
    pallas_call x1, Pallas kernels, fused_form(): pl.pallas_call(hand_on, out_shape=jax.ShapeDtypeStruct((probe_count, 1, o...  1.38 us

profile of v2, /device:TPU:0, one launch (start us, length us, event | category | flops | bytes accessed | tf_op | source)
XLA Modules:
  0.0 22.6 jit_solution(3865097884250225615)
XLA Ops:
  0.7 20.6 %shard_map.91.value = f32[16,512]{1,0:T(8,128)} custom-call(bf16[16,512]{1,0:T(8,128)(2,1)} %bitcast.3, s32[1,512]{1,0:T(1,128)} %level_in.1, f32[16]{0:T(128)} %table_in.1, bf16[2304,2048]{1,0:T(8,128)(2,1)} %bitcast.2, f32[6,384]{1,0:T(8,128)} %weight_in.1, s32[1,256]{1,0:T(1,128)} %first_in.1, s32[1,256]{1,0:T(1,128)} %second_in.1, f32[1,256]{1,0:T(1,128)} %coef_in.1, ...), custom_call_target="tpu_custom_call" | custom-call | flops 301989888 | bytes 9437184 | tf_op jit(solution)/shard_map/pallas_call | solution.py:351
  21.2 1.4 %shard_map.92 = f32[16,1,512]{2,1,0:T(1,128)} custom-call(f32[16,512]{1,0:T(8,128)} %shard_map.91.value), custom_call_target="tpu_custom_call" | custom-call | tf_op jit(solution)/shard_map/pallas_call | solution.py:407

commit v3 on v2

--- a/solution.py
+++ b/solution.py
@@ -229,7 +229,7 @@
 
     pl.semaphore_wait(barrier, nblk)
     mine = w_buf.at[:, block(blk)]
-    gathers = [to_blk(mine, mine, gather_sem, blk, peer) for peer in reversed(peers)]
+    gathers = [to_blk(mine, mine, gather_sem, blk, peer) for peer in peers]
     for copy in gathers:
         copy.start()
     asks = [to_other(second, asked, ask_sem, 0), to_other(strength, asked_strength, ask_sem, 1)]
@@ -299,13 +299,11 @@
     flux_pair = in_two(jnp.concatenate([flux, -flux, -far_flux], axis=1))
     spread = mxu(flux_pair, hot[...], NT)
     spread = spread[:probe_count] + spread[probe_count:]
-    swaps[0].wait_recv()
-    acc[...] = spread + mxu(residual_of(0), s_buf[rows(0), :])
-
-    for copy in swaps[1:]:
+    acc[...] = spread
+    for copy in swaps:
         copy.wait_recv()
-    late = jnp.concatenate([residual_of(k) for k in range(1, CHUNKS)], axis=1)
-    late_rows = pl.ds(chunk_rows, (CHUNKS - 1) * chunk_rows)
+    late = jnp.concatenate([residual_of(k) for k in range(CHUNKS)], axis=1)
+    late_rows = pl.ds(0, CHUNKS * chunk_rows)
     sums = []
     for place, peer in enumerate(reversed(peers)):
         term = acc[:, block(peer)] + mxu(late, s_buf[late_rows, block(peer)])
@@ -351,7 +349,7 @@
     result = pl.pallas_call(
         fused_kernel,
         out_shape=jax.ShapeDtypeStruct((probe_count, own_cells), f32),
-        in_specs=[pl.BlockSpec(memory_space=pl.ANY)] * 9,
+        in_specs=[pl.BlockSpec(memory_space=pltpu.HBM)] * 9,
         out_specs=vmem,
         scratch_shapes=[
             pltpu.VMEM((probe_count, own_cells), bf16),

time: 22.8 us -> 21.8 us (0.956)
  Pallas kernels: 22 us -> 21 us
    pallas_call x1, Pallas kernels: 20.6 us -> 19.6 us  [fused_form(): pl.pallas_call(fused_kernel, out_shape=jax.ShapeDtypeStruct((probe_count,...]
where the time goes in v3:
time: 21.8 us; the launch traced here: 21.6 us
  Pallas kernels  21 us (96%)
  between operations  0.66 us (3%)
    pallas_call x1, Pallas kernels, fused_form(): pl.pallas_call(fused_kernel, out_shape=jax.ShapeDtypeStruct((probe_count,...  19.6 us
    pallas_call x1, Pallas kernels, fused_form(): pl.pallas_call(hand_on, out_shape=jax.ShapeDtypeStruct((probe_count, 1, o...  1.38 us

profile of v3, /device:TPU:0, one launch (start us, length us, event | category | flops | bytes accessed | tf_op | source)
XLA Modules:
  0.0 21.6 jit_solution(4594004030661273464)
XLA Ops:
  0.7 19.6 %shard_map.91.value = f32[16,512]{1,0:T(8,128)} custom-call(bf16[16,512]{1,0:T(8,128)(2,1)} %bitcast.3, s32[1,512]{1,0:T(1,128)} %level_in.1, f32[16]{0:T(128)} %table_in.1, bf16[2304,2048]{1,0:T(8,128)(2,1)} %bitcast.2, f32[6,384]{1,0:T(8,128)} %weight_in.1, s32[1,256]{1,0:T(1,128)} %first_in.1, s32[1,256]{1,0:T(1,128)} %second_in.1, f32[1,256]{1,0:T(1,128)} %coef_in.1, ...), custom_call_target="tpu_custom_call" | custom-call | flops 301989888 | bytes 9437184 | tf_op jit(solution)/shard_map/pallas_call | solution.py:349
  20.2 1.4 %shard_map.92 = f32[16,1,512]{2,1,0:T(1,128)} custom-call(f32[16,512]{1,0:T(8,128)} %shard_map.91.value), custom_call_target="tpu_custom_call" | custom-call | tf_op jit(solution)/shard_map/pallas_call | solution.py:405
